TPU v7x, 32 devices: a whole 2x2x4 slice. The times are simulated.
32 devices in a mesh: svc: 16 (over z, y, core), tm: 2 (over x).
Axes of the slice: x: 2, y: 2, z: 4, core: 2. Of those that a mesh axis runs over, the one named last changes fastest.
Arguments:
- metrics: bfloat16 [8192, 4096], P('svc', 'tm'), may hold values from -15 to 15
- band_starts: int32 [4], replicated, may hold values from 1 to 2015
Outputs:
- cross: bfloat16 [4, 2, 8192, 8192], P(None, None, 'svc', 'tm')
- coherence: float32 [4, 8192, 8192], P(None, 'svc', 'tm')
Inputs may be any that keep to these rules, and one draw needn't show every extreme that they name: `band_starts`: each band covers 32 consecutive bins starting at its entry.
All inputs are finite; a program needn't handle non-finite values.
Results may differ from a plain program's by a relative error of at most 0.0066.
Values may be sent and summed in bfloat16 or wider, within the bound.
A program may use at most 192 MiB of HBM per device.

v0:
```python
import jax
import jax.numpy as jnp
from jax import lax
from jax.sharding import PartitionSpec as P

TLEN = 4096
BANDS = 4
BINS = 32


epsilon = 1e-06


def make_table(minutes, band_starts):
    offsets = jnp.arange(BINS, dtype=jnp.int32)
    freqs = band_starts[:, None] + offsets[None, :]
    phase_index = minutes[:, None, None] * freqs[None, :, :] % TLEN
    phases = 2.0 * jnp.pi / TLEN * phase_index.astype(jnp.float32)
    norm = 1.0 / jnp.sqrt(jnp.float32(TLEN))
    stacked = jnp.stack([jnp.cos(phases) * norm, -jnp.sin(phases) * norm], axis=2)
    return stacked.reshape(minutes.shape[0], BANDS * 2 * BINS).astype(jnp.bfloat16)


def band_products(row_spec, col_spec):
    swapped = jnp.concatenate([row_spec[:, BINS:], -row_spec[:, :BINS]], axis=1)
    dims = (((1,), (1,)), ((), ()))
    real_part = lax.dot_general(row_spec, col_spec, dims, preferred_element_type=jnp.float32) / BINS
    imag_part = lax.dot_general(swapped, col_spec, dims, preferred_element_type=jnp.float32) / BINS
    row_power = jnp.sum(jnp.square(row_spec.astype(jnp.float32)), axis=1) / BINS
    col_power = jnp.sum(jnp.square(col_spec.astype(jnp.float32)), axis=1) / BINS
    coherence = (real_part * real_part + imag_part * imag_part) / (
        (row_power[:, None] + epsilon) * (col_power[None, :] + epsilon)
    )
    cross = jnp.stack([real_part, imag_part], axis=0).astype(jnp.bfloat16)
    return (cross, coherence)


def body(metrics, band_starts):
    row_count = metrics.shape[0]
    local_minutes = metrics.shape[1]
    time_index = lax.axis_index("tm")
    minutes = time_index * local_minutes + jnp.arange(local_minutes, dtype=jnp.int32)
    dft_table = make_table(minutes, band_starts)
    partial_value = jnp.dot(metrics, dft_table, preferred_element_type=jnp.float32)
    spectra = lax.psum(partial_value, "tm").astype(jnp.bfloat16)
    owners = lax.axis_size("svc") // lax.axis_size("tm")
    col_count = row_count * owners
    gathered = lax.all_gather(spectra, "svc", axis=0, tiled=True)
    columns_panel = lax.dynamic_slice_in_dim(gathered, time_index * col_count, col_count, 0)
    cross_list = []
    coherence_list = []
    for band in range(BANDS):
        offset = band * 2 * BINS
        row_spec = spectra[:, offset : offset + 2 * BINS]
        col_spec = columns_panel[:, offset : offset + 2 * BINS]
        cross, coherence = band_products(row_spec, col_spec)
        cross_list.append(cross)
        coherence_list.append(coherence)
    return (jnp.stack(cross_list, axis=0), jnp.stack(coherence_list, axis=0))


def solution(mesh):
    return jax.shard_map(
        body,
        mesh=mesh,
        in_specs=(P("svc", "tm"), P()),
        out_specs=(P(None, None, "svc", "tm"), P(None, "svc", "tm")),
        check_vma=False,
    )
```

profile of v0, /device:TPU:3, one launch (start us, length us, event | category | flops | bytes accessed | tf_op | source)
XLA Modules:
  0.0 184.1 jit_solution(10810867141132946729)
XLA Ops:
  7.2 0.0 copy-start
  7.2 0.0 all-gather.2.cloned.1.call-start
  7.2 0.9 iota_add_fusion.1
  8.1 4.5 %multiply_convert_fusion.9 = (bf16[2048,4,1,32]{0,3,2,1:T(8,128)(2,1)S(1)}, bf16[2048,4,1,32]{0,3,2,1:T(8,128)(2,1)S(1)}) fusion(s32[4,32]{1,0:T(4,128)S(1)} %iota_add_fusion.1, s32[2048]{0:T(1024)S(1)} %iota_add_fusion), kind=kLoop, calls=%fused_computation.37 | loop fusion | flops 4980736 | bytes 1057280 | tf_op jit(solution)/shard_map/convert.16
  12.6 0.1 pad_maximum_fusion.1
  12.7 0.7 convolution_bitcast_fusion
  13.5 15.5 %all-reduce.1 = bf16[512,256]{0,1:T(8,128)(2,1)} all-reduce(f32[512,256]{0,1:T(8,128)S(1)} %convolution_bitcast_fusion), channel_id=1, replica_groups=mesh['svc'=16,'tm'=2] {'tm'}, use_global_device_ids=true, to_apply=%region_0.1 | all-reduce | flops 131072 | bytes 786432 | tf_op jit(solution)/shard_map/psum | solution.py:45
  29.0 0.0 all-gather.2.cloned.1.call-update
  29.0 1.0 multiply_reduce_fusion.7
  30.1 0.9 fusion.49
  31.0 54.2 %all-gather.2.cloned.1.call-done = bf16[8192,256]{0,1:T(8,128)(2,1)} async-done(((bf16[512,256]{0,1:T(8,128)(2,1)}), bf16[8192,256]{0,1:T(8,128)(2,1)}) %all-gather.2.cloned.1.call-update) | async-done | bytes 4194320 | tf_op jit(solution)/shard_map/all_gather | solution.py:48
  85.2 2.0 %multiply_reduce_fusion.3 = (f32[4096]{0:T(1024)S(1)}, f32[4096]{0:T(1024)S(1)}, f32[4096]{0:T(1024)S(1)}, f32[4096]{0:T(1024)S(1)}) fusion(bf16[8192,256]{0,1:T(8,128)(2,1)} %all-gather.2.cloned.1.call-done, s32[]{:T(128)S(6)} %select_n.22, s32[]{:T(128)S(6)} %add.144, s32[]{:T(128)S(6)} %add.145, s32[]{:T(128)S(6)} %add.146), kind=kLoop, calls=%fused_computation.35 | loop fusion | flops 3129344 | bytes 2162704 | tf_op jit(solution)/shard_map/reduce_sum | solution.py:30
  87.3 2.3 %fusion.11 = f32[512,4096]{1,0:T(8,128)S(1)} fusion(bf16[8192,256]{0,1:T(8,128)(2,1)} %all-gather.2.cloned.1.call-done, s32[]{:T(128)S(6)} %select_n.22, bf16[512,32]{0,1:T(8,128)(2,1)S(1)} %get-tuple-element.29, bf16[512,32]{0,1:T(8,128)(2,1)S(1)} %get-tuple-element.22), kind=kOutput, calls=%fused_computation.38 | convolution fusion | flops 268566528 | bytes 8978436 | tf_op jit(solution)/shard_map/dot_general | solution.py:28
  89.6 2.3 %fusion.15 = f32[512,4096]{1,0:T(8,128)S(1)} fusion(bf16[8192,256]{0,1:T(8,128)(2,1)} %all-gather.2.cloned.1.call-done, s32[]{:T(128)S(6)} %select_n.22, s32[]{:T(128)S(6)} %add.146, bf16[512,32]{0,1:T(8,128)(2,1)S(1)} %get-tuple-element.23, bf16[512,32]{0,1:T(8,128)(2,1)S(1)} %get-tuple-element.24), kind=kOutput, calls=%fused_computation.42 | convolution fusion | flops 268566528 | bytes 8978440 | tf_op jit(solution)/shard_map/dot_general | solution.py:28
  91.9 0.0 copy-start.3
  92.0 2.4 %fusion.23 = f32[512,4096]{1,0:T(8,128)S(1)} fusion(bf16[8192,256]{0,1:T(8,128)(2,1)} %all-gather.2.cloned.1.call-done, s32[]{:T(128)S(6)} %select_n.22, s32[]{:T(128)S(6)} %add.144, bf16[512,32]{0,1:T(8,128)(2,1)S(1)} %get-tuple-element.27, bf16[512,32]{0,1:T(8,128)(2,1)S(1)} %get-tuple-element.28), kind=kOutput, calls=%fused_computation.50 | convolution fusion | flops 268566528 | bytes 8978440 | tf_op jit(solution)/shard_map/dot_general | solution.py:28
  94.3 5.7 %fusion.19 = f32[512,4096]{1,0:T(8,128)} fusion(bf16[8192,256]{0,1:T(8,128)(2,1)} %all-gather.2.cloned.1.call-done, s32[]{:T(128)S(6)} %select_n.22, s32[]{:T(128)S(6)} %add.145, bf16[512,32]{0,1:T(8,128)(2,1)S(1)} %get-tuple-element.25, bf16[512,32]{0,1:T(8,128)(2,1)S(1)} %get-tuple-element.26), kind=kOutput, calls=%fused_computation.46 | convolution fusion | flops 268566528 | bytes 8978440 | tf_op jit(solution)/shard_map/dot_general | solution.py:28
  100.0 8.3 %divide_bitcast_fusion.3 = (f32[1,512,4096]{2,1,0:T(8,128)}, bf16[1,1,512,4096]{3,2,1,0:T(8,128)(2,1)}, bf16[1,1,512,4096]{3,2,1,0:T(8,128)(2,1)}) fusion(f32[512,4096]{1,0:T(8,128)S(1)} %fusion.11, f32[4096]{0:T(1024)S(1)} %get-tuple-element.35, f32[512]{0:T(512)S(1)} %get-tuple-element.39, bf16[8192,256]{0,1:T(8,128)(2,1)} %all-gather.2.cloned.1.call-done, ...), kind=kOutput, calls=%fused_computation.5 | convolution fusion | flops 287309824 | bytes 25774084 | tf_op jit(solution)/shard_map/dot_general | solution.py:27
  108.4 9.8 %divide_bitcast_fusion.1 = (f32[1,512,4096]{2,1,0:T(8,128)}, bf16[1,1,512,4096]{3,2,1,0:T(8,128)(2,1)}, bf16[1,1,512,4096]{3,2,1,0:T(8,128)(2,1)}) fusion(f32[512,4096]{1,0:T(8,128)} %fusion.19, f32[4096]{0:T(1024)S(1)} %get-tuple-element.33, f32[512]{0:T(512)S(1)} %get-tuple-element.37, bf16[8192,256]{0,1:T(8,128)(2,1)} %all-gather.2.cloned.1.call-done, ...), kind=kOutput, calls=%fused_computation.3 | convolution fusion | flops 287309824 | bytes 25774088 | tf_op jit(solution)/shard_map/dot_general | solution.py:27
  118.1 8.5 %divide_bitcast_fusion.2 = (f32[1,512,4096]{2,1,0:T(8,128)}, bf16[1,1,512,4096]{3,2,1,0:T(8,128)(2,1)}, bf16[1,1,512,4096]{3,2,1,0:T(8,128)(2,1)}) fusion(f32[512,4096]{1,0:T(8,128)S(1)} %fusion.23, f32[4096]{0:T(1024)S(1)} %get-tuple-element.34, f32[512]{0:T(512)S(1)} %get-tuple-element.38, bf16[8192,256]{0,1:T(8,128)(2,1)} %all-gather.2.cloned.1.call-done, ...), kind=kOutput, calls=%fused_computation.4 | convolution fusion | flops 287309824 | bytes 25774088 | tf_op jit(solution)/shard_map/dot_general | solution.py:27
  126.6 9.2 %divide_bitcast_fusion = (f32[1,512,4096]{2,1,0:T(8,128)}, bf16[1,1,512,4096]{3,2,1,0:T(8,128)(2,1)}, bf16[1,1,512,4096]{3,2,1,0:T(8,128)(2,1)}) fusion(f32[512,4096]{1,0:T(8,128)S(1)} %fusion.15, f32[4096]{0:T(1024)S(1)} %get-tuple-element.32, f32[512]{0:T(512)S(1)} %get-tuple-element.36, bf16[8192,256]{0,1:T(8,128)(2,1)} %all-gather.2.cloned.1.call-done, ...), kind=kOutput, calls=%fused_computation.2 | convolution fusion | flops 287309824 | bytes 25774088 | tf_op jit(solution)/shard_map/dot_general | solution.py:27
  135.8 18.5 %pad_maximum_fusion = f32[4,512,4096]{2,1,0:T(8,128)} fusion(f32[1,512,4096]{2,1,0:T(8,128)} %get-tuple-element.19, f32[1,512,4096]{2,1,0:T(8,128)S(1)} %copy-done.2, f32[1,512,4096]{2,1,0:T(8,128)} %get-tuple-element.13, f32[1,512,4096]{2,1,0:T(8,128)S(1)} %bitcast.30), kind=kLoop, calls=%fused_computation.1 | loop fusion | flops 25165824 | bytes 67108864 | tf_op jit(solution)/shard_map/stack | solution.py:59
  154.3 22.9 %maximum_maximum_fusion = bf16[4,2,512,4096]{3,2,1,0:T(8,128)(2,1)} fusion(bf16[1,1,512,4096]{3,2,1,0:T(8,128)(2,1)} %get-tuple-element.21, bf16[1,1,512,4096]{3,2,1,0:T(8,128)(2,1)} %get-tuple-element.20, bf16[1,1,512,4096]{3,2,1,0:T(8,128)(2,1)} %get-tuple-element.18, bf16[1,1,512,4096]{3,2,1,0:T(8,128)(2,1)} %get-tuple-element.17, ...), kind=kLoop, calls=%fused_computation | loop fusion | flops 117440512 | bytes 67108864 | tf_op jit(solution)/shard_map/stack | solution.py:59
  177.2 0.0 copy-done.1
  (15 shorter events, 0.0 us)
Async XLA Ops:
  7.2 5.6 %copy-start = (bf16[512,2048]{1,0:T(8,128)(2,1)S(1)}, bf16[512,2048]{1,0:T(8,128)(2,1)}, u32[]{:S(2)}) copy-start(bf16[512,2048]{1,0:T(8,128)(2,1)} %param.2) | copy-start | bytes 6291460
  7.2 78.0 %all-gather.2.cloned.1.call-start = ((), (), s32[]{:S(2)}) async-start(), calls=%async_computation | async-start | bytes 4456448 | tf_op jit(solution)/shard_map/all_gather | solution.py:48
  91.9 8.1 %copy-start.3 = (bf16[512,256]{0,1:T(8,128)(2,1)S(1)}, bf16[512,256]{0,1:T(8,128)(2,1)}, u32[]{:S(2)}) copy-start(bf16[512,256]{0,1:T(8,128)(2,1)} %all-reduce.1) | copy-start | bytes 786436
  118.1 17.7 %slice-start = ((s8[8388608]{0:T(1024)(128)(4,1)}), s8[4194304]{0:T(1024)(128)(4,1)S(1)}, s32[]{:S(2)}) async-start(s8[8388608]{0:T(1024)(128)(4,1)} %bitcast.29), calls=%async_computation.1 | async-start | bytes 8388608
  126.6 9.2 %slice-start.1 = ((s8[8388608]{0:T(1024)(128)(4,1)}), s8[4194304]{0:T(1024)(128)(4,1)S(1)}, s32[]{:S(2)}) async-start(s8[8388608]{0:T(1024)(128)(4,1)} %bitcast.29), calls=%async_computation.2 | async-start | bytes 8388608
  126.6 9.2 %copy-start.2 = (f32[1,512,4096]{2,1,0:T(8,128)S(1)}, f32[1,512,4096]{2,1,0:T(8,128)}, u32[]{:S(2)}) copy-start(f32[1,512,4096]{2,1,0:T(8,128)} %get-tuple-element.16) | copy-start | bytes 25165828
  154.3 22.9 %copy-start.1 = (bf16[512,2048]{1,0:T(8,128)(2,1)S(1)}, bf16[512,2048]{1,0:T(8,128)(2,1)}, u32[]{:S(2)}) copy-start(bf16[512,2048]{1,0:T(8,128)(2,1)} %param.2) | copy-start | bytes 6291460
Sparse Core Ops, SparseCore 0:
  29.2 56.0 all-gather.1
where the time goes:
time: 186 us; the launch traced here: 184 us
  waiting for transfers between devices  54.3 us (29%)
  other arithmetic  50.9 us (27%)
  matrix products  49.2 us (26%)
  blocking collectives  15.5 us (8%)
  between operations  14.2 us (8%)
    all_gather x1, waiting for transfers between devices, body(): gathered = lax.all_gather(spectra, 'svc', axis=0, tiled=True)  54.2 us
    another operation x2, other arithmetic, body(): return (jnp.stack(cross_list, axis=0), jnp.stack(coherence_list, axis=0))  41.4 us
    dot_general x4, matrix products, band_products(): lax.dot_general(row_spec, col_spec, dims, preferred_element_type=jnp.floa...  35.7 us
    psum x1, blocking collectives, body(): spectra = lax.psum(partial_value, 'tm').astype(jnp.bfloat16)  15.5 us
    dot_general x4, matrix products, band_products(): lax.dot_general(swapped, col_spec, dims, preferred_element_type=jnp.float32)  12.7 us
    another operation x1, other arithmetic  4.5 us
  transfers between devices with their start and end apart: 1, of which 1 were waited for; matrix products, arithmetic and copies ran while one was open for 1% of the time, Pallas kernels for 0%

commit v1 on v0

v1 whole, which is shorter than its diff:
```python
import functools
import math

import jax
import jax.numpy as jnp
from jax import lax
from jax.experimental import pallas as pl
from jax.experimental.pallas import tpu as pltpu
from jax.sharding import PartitionSpec as P

BANDS = 4
BINS = 32
WIDTH = BANDS * 2 * BINS
EPSILON = 1e-06
SPLIT = 64
CHUNKS = 2
LAG = 2
MESH = pl.DeviceIdType.MESH
NT = (((1,), (1,)), ((), ()))


def fill_table(table, starts, first_minute, tlen):
    minutes = table.shape[0]
    lane = lax.broadcasted_iota(jnp.int32, (1, WIDTH), 1)
    band = lane // (2 * BINS)
    start = jnp.zeros((1, WIDTH), jnp.int32)
    for b in range(BANDS):
        start = jnp.where(band == b, starts[b], start)
    freq = start + lane % BINS
    quarter = (lane // BINS) % 2 * (tlen // 4)
    unit = 2.0 * math.pi / tlen
    outer = minutes // SPLIT
    ta = first_minute + SPLIT * lax.broadcasted_iota(jnp.int32, (outer, WIDTH), 0)
    angle_a = ((ta * freq) & (tlen - 1)).astype(jnp.float32) * unit
    tb = lax.broadcasted_iota(jnp.int32, (SPLIT, WIDTH), 0)
    angle_b = ((tb * freq + quarter) & (tlen - 1)).astype(jnp.float32) * unit
    norm = 1.0 / math.sqrt(tlen)
    cos_a, sin_a = jnp.cos(angle_a), jnp.sin(angle_a)
    cos_b, sin_b = jnp.cos(angle_b) * norm, jnp.sin(angle_b) * norm
    for a in range(outer):
        rows = cos_a[a : a + 1] * cos_b - sin_a[a : a + 1] * sin_b
        table[a * SPLIT : (a + 1) * SPLIT, :] = rows.astype(jnp.bfloat16)


def spectra_kernel(
    S, T, starts, metrics_hbm, cols, lhs, rinv,
    metrics, table, partial, landed, rows,
    in_sem, rs_send, rs_recv, ag_send, ag_recv, up_send, down_send, z_recv, y_send, y_recv, c_send, c_recv,
):
    s, t = lax.axis_index("svc"), lax.axis_index("tm")
    R, L = metrics.shape
    piece = R // T
    size = piece // CHUNKS
    Z, ZP = S // 4, S // T // 4
    z, y, c = s // 4, (s // 2) % 2, s % 2
    z0 = t * ZP
    own_z = z - z0
    in_panel = (own_z >= 0) & (own_z < ZP)
    near = jnp.clip(own_z, 0, ZP - 1)
    y_mate = (z * 4 + (1 - y) * 2 + c, t)
    c_mate = (z * 4 + y * 2 + 1 - c, t)
    z_up = (lax.rem(z + 1, Z) * 4 + y * 2 + c, t)
    z_down = (lax.rem(z + Z - 1, Z) * 4 + y * 2 + c, t)

    load = pltpu.make_async_copy(metrics_hbm, metrics, in_sem)
    load.start()
    barrier = pltpu.get_barrier_semaphore()
    for i in range(1, T):
        pl.semaphore_signal(barrier, inc=1, device_id=(s, lax.rem(t + i, T)), device_id_type=MESH)
    for mate in (y_mate, c_mate, z_up, z_down):
        pl.semaphore_signal(barrier, inc=1, device_id=mate, device_id_type=MESH)

    fill_table(table, starts, t * L, T * L)
    load.wait()

    def transform(first):
        return jnp.dot(metrics[pl.ds(first, size), :], table[...], preferred_element_type=jnp.float32)

    def remote(src, dst, send, recv, to):
        return pltpu.make_async_remote_copy(
            src_ref=src, dst_ref=dst, send_sem=send, recv_sem=recv, device_id=to, device_id_type=MESH
        )

    def rs_copy(i, ch):
        part = pl.ds(ch * size, size)
        to = (s, lax.rem(t + 1 + i, T))
        return remote(partial.at[i, part], landed.at[i, part], rs_send.at[i, ch], rs_recv.at[i, ch], to)

    for i in range(T - 1):
        for ch in range(CHUNKS):
            target = lax.rem(t + 1 + i, T)
            partial[i, pl.ds(ch * size, size), :] = transform(pl.multiple_of(target * piece + ch * size, size))
            if i == 0 and ch == 0:
                pl.semaphore_wait(barrier, T - 1 + 4)
            rs_copy(i, ch).start()
    for ch in range(CHUNKS):
        partial[T - 1, pl.ds(ch * size, size), :] = transform(pl.multiple_of(t * piece + ch * size, size))

    def row_part(h, ch):
        return pl.ds(pl.multiple_of(h * piece + ch * size, size), size)

    def ag_copy(i, ch):
        to = (s, lax.rem(t + 1 + i, T))
        part = rows.at[row_part(t, ch)]
        return remote(part, part, ag_send.at[i, ch], ag_recv.at[i, ch], to)

    def unit(zs, i, ch, yy, cc):
        h = lax.rem(t + T - i, T)
        return pl.ds(pl.multiple_of((zs * 4 + yy * 2 + cc) * R + h * piece + ch * size, size), size)

    def uid(zs, i, ch):
        return (zs * T + i) * CHUNKS + ch

    def z_copy(zs, i, ch, sems, to):
        n = uid(zs, i, ch)
        part = cols.at[unit(zs, i, ch, y, c)]
        return remote(part, part, sems.at[n], z_recv.at[n], to)

    def y_copy(zs, i, ch, yy):
        n = uid(zs, i, ch)
        part = cols.at[unit(zs, i, ch, yy, c)]
        return remote(part, part, y_send.at[n], y_recv.at[n], y_mate)

    def c_copy(zs, i, ch, yy, cc, other):
        n = uid(zs, i, ch)
        part = cols.at[unit(zs, i, ch, yy, cc)]
        return remote(part, part, c_send.at[other, n], c_recv.at[other, n], c_mate)

    def goes_up(zs):
        return (own_z >= zs) & (z < Z - 1)

    def goes_down(zs):
        return (own_z <= zs) & (z > 0)

    def forward(zs, i, ch):
        @pl.when(goes_up(zs))
        def _():
            z_copy(zs, i, ch, up_send, z_up).start()

        @pl.when(goes_down(zs))
        def _():
            z_copy(zs, i, ch, down_send, z_down).start()

        y_copy(zs, i, ch, y).start()
        c_copy(zs, i, ch, y, c, 0).start()

    for ch in range(CHUNKS):
        part = pl.ds(ch * size, size)
        total = partial[T - 1, part, :]
        for i in range(T - 1):
            rs_copy(i, ch).wait_recv()
            total = total + landed[i, part, :]
        rounded = total.astype(jnp.bfloat16)
        rows[row_part(t, ch), :] = rounded
        for i in range(T - 1):
            ag_copy(i, ch).start()

        @pl.when(in_panel)
        def _():
            cols[unit(near, 0, ch, y, c), :] = rounded
            forward(near, 0, ch)

    order = [(j, i, ch) for j in range(ZP) for i in range(T) for ch in range(CHUNKS)]

    def pass_on(k):
        j, i, ch = order[k]
        zs = lax.rem(near + j, ZP)
        y_copy(zs, i, ch, 1 - y).wait_recv()
        c_copy(zs, i, ch, 1 - y, c, 1).start()

    for k, (j, i, ch) in enumerate(order):
        zs = lax.rem(near + j, ZP)

        def arrive(zs=zs, i=i, ch=ch):
            z_copy(zs, i, ch, up_send, z_up).wait_recv()
            forward(zs, i, ch)

        if j:
            arrive()
        else:
            pl.when(jnp.logical_not(in_panel))(arrive)
            if i:

                @pl.when(in_panel)
                def _():
                    ag_copy(i - 1, ch).wait_recv()
                    cols[unit(zs, i, ch, y, c), :] = rows[row_part(lax.rem(t + T - i, T), ch), :]
                    forward(zs, i, ch)

        if k >= LAG:
            pass_on(k - LAG)

    @pl.when(jnp.logical_not(in_panel))
    def _():
        for i in range(T - 1):
            for ch in range(CHUNKS):
                ag_copy(i, ch).wait_recv()

    for k in range(max(len(order) - LAG, 0), len(order)):
        pass_on(k)

    lane = lax.broadcasted_iota(jnp.int32, (1, WIDTH), 1)
    x = rows[...].astype(jnp.float32)
    square = x * x
    high = square.astype(jnp.bfloat16)
    low = (square - high.astype(jnp.float32)).astype(jnp.bfloat16)
    x = x * (1.0 / BINS)
    swapped = jnp.where(
        (lane // BINS) % 2 == 0, pltpu.roll(x, WIDTH - BINS, 1), -pltpu.roll(x, BINS, 1)
    )
    entry = lax.broadcasted_iota(jnp.int32, (WIDTH, 128), 0) // (2 * BINS)
    for b in range(BANDS):
        here = lane // (2 * BINS) == b
        lhs[2 * b] = jnp.where(here, x, 0.0).astype(jnp.bfloat16)
        lhs[2 * b + 1] = jnp.where(here, swapped, 0.0).astype(jnp.bfloat16)
        ones = jnp.where(entry == b, 1.0, 0.0).astype(jnp.bfloat16)
        power = jnp.dot(high, ones, preferred_element_type=jnp.float32)
        power = power + jnp.dot(low, ones, preferred_element_type=jnp.float32)
        rinv[b] = 1.0 / (power * (1.0 / BINS) + EPSILON)

    for j, i, ch in order:
        zs = lax.rem(near + j, ZP)
        c_copy(zs, i, ch, y, 1 - c, 0).wait_recv()
        c_copy(zs, i, ch, 1 - y, 1 - c, 1).wait_recv()

    for i in range(T - 1):
        for ch in range(CHUNKS):
            rs_copy(i, ch).wait_send()
            ag_copy(i, ch).wait_send()
    for j, i, ch in order:
        zs = lax.rem(near + j, ZP)

        @pl.when(goes_up(zs))
        def _():
            z_copy(zs, i, ch, up_send, z_up).wait_send()

        @pl.when(goes_down(zs))
        def _():
            z_copy(zs, i, ch, down_send, z_down).wait_send()

        y_copy(zs, i, ch, y).wait_send()
        c_copy(zs, i, ch, y, c, 0).wait_send()
        c_copy(zs, i, ch, 1 - y, c, 1).wait_send()


def gather_spectra(S, T, metrics, band_starts):
    R, L = metrics.shape
    owners = S // T
    piece = R // T
    units = owners // 4 * T * CHUNKS
    dma = pltpu.SemaphoreType.DMA
    vmem = pl.BlockSpec(memory_space=pltpu.VMEM)
    return pl.pallas_call(
        functools.partial(spectra_kernel, S, T),
        out_shape=(
            jax.ShapeDtypeStruct((owners * R, WIDTH), jnp.bfloat16),
            jax.ShapeDtypeStruct((2 * BANDS, R, WIDTH), jnp.bfloat16),
            jax.ShapeDtypeStruct((BANDS, R, 128), jnp.float32),
        ),
        in_specs=[pl.BlockSpec(memory_space=pltpu.SMEM), pl.BlockSpec(memory_space=pl.ANY)],
        out_specs=(vmem, vmem, vmem),
        scratch_shapes=[
            pltpu.VMEM((R, L), jnp.bfloat16),
            pltpu.VMEM((L, WIDTH), jnp.bfloat16),
            pltpu.VMEM((T, piece, WIDTH), jnp.float32),
            pltpu.VMEM((T - 1, piece, WIDTH), jnp.float32),
            pltpu.VMEM((R, WIDTH), jnp.bfloat16),
            dma,
            dma((T - 1, CHUNKS)),
            dma((T - 1, CHUNKS)),
            dma((T - 1, CHUNKS)),
            dma((T - 1, CHUNKS)),
            dma((units,)),
            dma((units,)),
            dma((units,)),
            dma((units,)),
            dma((units,)),
            dma((2, units)),
            dma((2, units)),
        ],
        compiler_params=pltpu.CompilerParams(
            collective_id=0, has_side_effects=True, vmem_limit_bytes=40 * 1024 * 1024
        ),
        name="spectra",
    )(band_starts, metrics)


def products_kernel(lhs, rinv, cols, cross, coherence, cinv):
    tile = cols.shape[0]

    @pl.when(pl.program_id(1) == 0)
    def _():
        x = cols[...].astype(jnp.float32)
        square = x * x
        high = square.astype(jnp.bfloat16)
        low = (square - high.astype(jnp.float32)).astype(jnp.bfloat16)
        band = lax.broadcasted_iota(jnp.int32, (16, WIDTH), 0)
        lane = lax.broadcasted_iota(jnp.int32, (16, WIDTH), 1)
        ones = jnp.where(lane // (2 * BINS) == band, 1.0, 0.0).astype(jnp.bfloat16)
        power = lax.dot_general(ones, high, NT, preferred_element_type=jnp.float32)
        power = power + lax.dot_general(ones, low, NT, preferred_element_type=jnp.float32)
        cinv[...] = 1.0 / (power * (1.0 / BINS) + EPSILON)

    right = cols[...]
    for b in range(BANDS):
        real = lax.dot_general(lhs[2 * b], right, NT, preferred_element_type=jnp.float32)
        imag = lax.dot_general(lhs[2 * b + 1], right, NT, preferred_element_type=jnp.float32)
        cross[b, 0] = real.astype(jnp.bfloat16)
        cross[b, 1] = imag.astype(jnp.bfloat16)
        row_scale = jnp.concatenate([rinv[b]] * (tile // 128), axis=1)
        coherence[b] = (real * real + imag * imag) * row_scale * cinv[b : b + 1, :]


def products(lhs, rinv, cols):
    R, C = lhs.shape[1], cols.shape[0]
    high, wide = 128, 512
    return pl.pallas_call(
        products_kernel,
        grid=(C // wide, R // high),
        out_shape=(
            jax.ShapeDtypeStruct((BANDS, 2, R, C), jnp.bfloat16),
            jax.ShapeDtypeStruct((BANDS, R, C), jnp.float32),
        ),
        in_specs=[
            pl.BlockSpec((2 * BANDS, high, WIDTH), lambda j, i: (0, i, 0)),
            pl.BlockSpec((BANDS, high, 128), lambda j, i: (0, i, 0)),
            pl.BlockSpec((wide, WIDTH), lambda j, i: (j, 0)),
        ],
        out_specs=(
            pl.BlockSpec((BANDS, 2, high, wide), lambda j, i: (0, 0, i, j)),
            pl.BlockSpec((BANDS, high, wide), lambda j, i: (0, i, j)),
        ),
        scratch_shapes=[pltpu.VMEM((16, wide), jnp.float32)],
        compiler_params=pltpu.CompilerParams(vmem_limit_bytes=40 * 1024 * 1024),
        name="products",
    )(lhs, rinv, cols)


def solution(mesh):
    S, T = mesh.shape["svc"], mesh.shape["tm"]

    def body(metrics, band_starts):
        cols, lhs, rinv = gather_spectra(S, T, metrics, band_starts)
        return products(lhs, rinv, cols)

    return jax.shard_map(
        body,
        mesh=mesh,
        in_specs=(P("svc", "tm"), P()),
        out_specs=(P(None, None, "svc", "tm"), P(None, "svc", "tm")),
        check_vma=False,
    )
```

time: 186 us -> 74.7 us (0.40)
  Pallas kernels: 0 us -> 71.6 us
  waiting for transfers between devices: 54.3 us -> 0 us
  other arithmetic: 50.9 us -> 0 us
  matrix products: 49.2 us -> 0 us
  blocking collectives: 15.5 us -> 0 us
  between operations: 14.2 us -> 0.65 us
  local copies, waits for them, and re-layouts: 0.03 us -> 2.24 us
    pallas_call x0 -> x2, Pallas kernels: none -> 71.6 us  [the longest x1 38.8 us: products(): pl.pallas_call(products_kernel, grid=(C // wide, R // high), out_shape=(j...]
    all_gather x1 -> x0, waiting for transfers between devices: 54.2 us -> none  [body(): gathered = lax.all_gather(spectra, 'svc', axis=0, tiled=True)]
    dot_general x9 -> x0, matrix products: 49.2 us -> none  [the longest x4 35.7 us: band_products(): lax.dot_general(row_spec, col_spec, dims, preferred_element_type=jnp.floa...]
    another operation x4 -> x0, other arithmetic: 46 us -> none  [the longest x2 41.4 us: body(): return (jnp.stack(cross_list, axis=0), jnp.stack(coherence_list, axis=0))]
    psum x1 -> x0, blocking collectives: 15.5 us -> none  [body(): spectra = lax.psum(partial_value, 'tm').astype(jnp.bfloat16)]
    reduce_sum x2 -> x0, other arithmetic: 3.05 us -> none  [the longest x1 2.04 us: band_products(): col_power = jnp.sum(jnp.square(col_spec.astype(jnp.float32)), axis=1) / BINS]
    unnamed x12 -> x4, local copies, waits for them, and re-layouts: 0.03 us -> 2.24 us
  transfers between devices with their start and end apart: 1 -> 0, of which waited for: 1 -> 0; matrix products, arithmetic and copies ran while one was open for 1% -> 0% of each run, Pallas kernels for 0% -> 0%
where the time goes in v1:
time: 74.7 us; the launch traced here: 74.5 us
  Pallas kernels  71.6 us (96%)
  local copies, waits for them, and re-layouts  2.24 us (3%)
    pallas_call x1, Pallas kernels, products(): pl.pallas_call(products_kernel, grid=(C // wide, R // high), out_shape=(j...  38.8 us
    pallas_call x1, Pallas kernels, gather_spectra(): pl.pallas_call(functools.partial(spectra_kernel, S, T), out_shape=(jax.Sh...  32.8 us
    unnamed x4, local copies, waits for them, and re-layouts  2.24 us

profile of v1, /device:TPU:3, one launch (start us, length us, event | category | flops | bytes accessed | tf_op | source)
XLA Modules:
  0.0 74.5 jit_solution(12554223010779201534)
XLA Ops:
  0.6 0.0 copy-start
  0.6 1.6 %copy-done = bf16[512,2048]{1,0:T(8,128)(2,1)S(1)} copy-done((bf16[512,2048]{1,0:T(8,128)(2,1)S(1)}, bf16[512,2048]{1,0:T(8,128)(2,1)}, u32[]{:S(2)}) %copy-start) | copy-done | bytes 2097176
  2.2 0.0 copy-start.1
  2.2 0.7 copy-done.1
  2.9 32.8 %spectra.1 = (bf16[4096,256]{1,0:T(8,128)(2,1)S(1)}, bf16[8,512,256]{2,1,0:T(8,128)(2,1)S(1)}, f32[4,512,128]{2,1,0:T(8,128)S(1)}) custom-call(s32[4]{0:T(128)S(1)} %copy-done.1, bf16[512,2048]{1,0:T(8,128)(2,1)S(1)} %copy-done), custom_call_target="tpu_custom_call" | custom-call | tf_op jit(solution)/shard_map/spectra/pallas_call | solution.py:253
  35.7 38.8 %products.1 = (bf16[4,2,512,4096]{3,2,1,0:T(8,128)(2,1)}, f32[4,512,4096]{2,1,0:T(8,128)}) custom-call(bf16[8,512,256]{2,1,0:T(8,128)(2,1)S(1)} %get-tuple-element.5.lhs, f32[4,512,128]{2,1,0:T(8,128)S(1)} %get-tuple-element.6.rinv, bf16[4096,256]{1,0:T(8,128)(2,1)S(1)} %get-tuple-element.7.cols), custom_call_target="tpu_custom_call" | custom-call | tf_op jit(solution)/shard_map/products/pallas_call | solution.py:317
Async XLA Ops:
  0.6 1.6 %copy-start = (bf16[512,2048]{1,0:T(8,128)(2,1)S(1)}, bf16[512,2048]{1,0:T(8,128)(2,1)}, u32[]{:S(2)}) copy-start(bf16[512,2048]{1,0:T(8,128)(2,1)} %metrics_hbm.1) | copy-start | bytes 6291460
  2.2 0.7 copy-start.1
